TPU v7x, 256 devices: a whole 4x4x8 slice. The times are simulated.
256 devices in a mesh: row: 16 (over z, y_lo), col: 16 (over x, y_hi, core).
Axes of the slice: x: 4, y: 4 (y_hi: 2, y_lo: 2; y = y_hi * 2 + y_lo), z: 8, core: 2. Of those that a mesh axis runs over, the one named last changes fastest.
Arguments:
- grad: bfloat16 [8192, 4096], P('row', 'col'), may hold values from -6 to 6
- left_basis: bfloat16 [8192, 8192], P('col', 'row'), may hold values from -0.0625 to 0.0625
- right_basis: bfloat16 [4096, 4096], P('row', 'col'), may hold values from -0.09375 to 0.09375
- exp_avg: float32 [8192, 4096], P('row', 'col'), may hold values from -4 to 4
- exp_avg_sq: float32 [8192, 4096], P('row', 'col'), may hold values from 0.05 to 2
Outputs:
- update: float32 [8192, 4096], P('row', 'col')
- new_avg: float32 [8192, 4096], P('row', 'col')
- new_sq: float32 [8192, 4096], P('row', 'col')
All inputs are finite; a program needn't handle non-finite values.
Results may differ from a plain program's by a relative error of at most 0.0041.
Values may be sent and summed in bfloat16 or wider, within the bound.
A program may use at most 64 MiB of HBM per device.

v0:
```python
import jax
import jax.numpy as jnp
from jax import lax
from jax.sharding import PartitionSpec as P

STEP = 10


beta_first = 0.95
beta_second = 0.95
epsilon = 1e-08


def shards(grad, left_basis, right_basis, exp_avg, exp_avg_sq):
    grad_cols, right_cols = (
        lax.all_gather(grad, "row", axis=0, tiled=True),
        lax.all_gather(right_basis, "row", axis=0, tiled=True),
    )
    inner = (((0,), (0,)), ((), ()))
    window_rows = grad_cols
    rotated = lax.dot_general(
        lax.all_gather(left_basis, "col", axis=0, tiled=True),
        window_rows,
        inner,
        preferred_element_type=jnp.float32,
    )
    rotated = rotated.astype(jnp.bfloat16)
    window_rows = right_cols
    projected = jnp.dot(
        lax.all_gather(rotated, "col", axis=1, tiled=True),
        window_rows,
        preferred_element_type=jnp.float32,
    )
    new_avg = beta_first * exp_avg + (1.0 - beta_first) * projected
    new_sq = beta_second * exp_avg_sq + (1.0 - beta_second) * projected * projected
    first_fix = 1.0 - beta_first**STEP
    second_fix = 1.0 - beta_second**STEP
    direction = (new_avg / first_fix / (jnp.sqrt(new_sq / second_fix) + epsilon)).astype(
        jnp.bfloat16
    )
    whole = jnp.dot(
        lax.all_gather(left_basis, "col", axis=0, tiled=True),
        direction,
        preferred_element_type=jnp.float32,
    )
    back = lax.psum_scatter(whole, "row", scatter_dimension=0, tiled=True)
    back = back.astype(jnp.bfloat16)
    outer = (((1,), (1,)), ((), ()))
    spread = lax.dot_general(back, right_cols, outer, preferred_element_type=jnp.float32)
    update = lax.psum_scatter(spread, "col", scatter_dimension=1, tiled=True)
    return (update, new_avg, new_sq)


def solution(mesh):
    return jax.shard_map(
        shards,
        mesh=mesh,
        in_specs=(
            P("row", "col"),
            P("col", "row"),
            P("row", "col"),
            P("row", "col"),
            P("row", "col"),
        ),
        out_specs=(P("row", "col"), P("row", "col"), P("row", "col")),
        check_vma=False,
    )
```

profile of v0, /device:TPU:10, one launch (start us, length us, event | category | flops | bytes accessed | tf_op | source)
XLA Modules:
  0.0 645.5 jit_solution(10451973779268098513)
XLA Ops:
  7.2 0.0 all-gather.7.cloned.1.call-start
  7.2 0.7 all-gather.7.cloned.1.call-update
  7.9 0.0 all-gather.5.cloned.1.call-start
  7.9 0.7 all-gather.5.cloned.1.call-update
  8.6 0.0 all-gather.11.cloned.1.call-start
  8.7 0.7 all-gather.11.cloned.1.call-update
  9.4 0.0 copy-start.4
  9.4 0.0 copy-start.5
  9.4 0.0 all-gather.9.cloned.1.call-start
  9.4 101.8 %all-gather.7.cloned.1.call-done = bf16[8192,256]{1,0:T(8,128)(2,1)} async-done(((bf16[512,256]{1,0:T(8,128)(2,1)}), bf16[8192,256]{1,0:T(8,128)(2,1)}) %all-gather.7.cloned.1.call-update) | async-done | bytes 4194320 | tf_op jit(solution)/shard_map/all_gather | solution.py:16
  111.2 79.0 %all-gather.5.cloned.1.call-done = bf16[8192,512]{1,0:T(8,128)(2,1)} async-done(((bf16[512,512]{1,0:T(8,128)(2,1)}), bf16[8192,512]{1,0:T(8,128)(2,1)}) %all-gather.5.cloned.1.call-update) | async-done | bytes 8388624 | tf_op jit(solution)/shard_map/all_gather | solution.py:42
  190.3 7.7 %convolution_convert_fusion = bf16[512,256]{1,0:T(8,128)(2,1)} fusion(bf16[8192,512]{1,0:T(8,128)(2,1)} %all-gather.5.cloned.1.call-done, bf16[8192,256]{1,0:T(8,128)(2,1)} %all-gather.7.cloned.1.call-done), kind=kOutput, calls=%fused_computation.1 | convolution fusion | flops 2147614720 | bytes 12845056 | tf_op jit(solution)/shard_map/dot_general | solution.py:21
  197.9 0.0 all-gather.9.cloned.1.call-update
  197.9 0.0 reduce-scatter.3.cloned.1.call-start
  198.0 65.8 %all-gather.11.cloned.1.call-done = bf16[4096,256]{1,0:T(8,128)(2,1)} async-done(((bf16[256,256]{1,0:T(8,128)(2,1)}), bf16[4096,256]{1,0:T(8,128)(2,1)}) %all-gather.11.cloned.1.call-update) | async-done | bytes 2097168 | tf_op jit(solution)/shard_map/all_gather | solution.py:17
  263.8 65.2 %all-gather.9.cloned.1.call-done = bf16[512,4096]{1,0:T(8,128)(2,1)} async-done(((bf16[512,256]{1,0:T(8,128)(2,1)}), bf16[512,4096]{1,0:T(8,128)(2,1)}) %all-gather.9.cloned.1.call-update) | async-done | bytes 4194320 | tf_op jit(solution)/shard_map/all_gather | solution.py:30
  329.0 0.0 copy-done.4
  329.0 0.0 copy-done.5
  329.0 0.0 copy-start
  329.0 4.3 multiply_add_fusion
  333.3 0.0 copy-start.2
  333.3 0.0 copy-start.3
  333.3 1.0 copy-done
  334.3 5.9 convolution_bitcast_fusion
  340.2 0.0 copy-done.2
  340.2 0.0 copy-done.3
  340.2 0.0 copy-start.1
  340.2 0.0 reduce-scatter.3.cloned.1.call-update
  340.2 0.0 reduce-scatter.5.cloned.1.call-start
  340.2 181.7 %reduce-scatter.3.cloned.1.call-done = f32[512,256]{0,1:T(8,128)} async-done(((f32[8192,256]{0,1:T(8,128)}), f32[512,256]{0,1:T(8,128)}) %reduce-scatter.3.cloned.1.call-update) | async-done | bytes 524304 | tf_op jit(solution)/shard_map/reduce_scatter | solution.py:46
  522.0 0.0 copy-done.1
  522.0 5.6 fusion.1
  527.6 0.0 reduce-scatter.5.cloned.1.call-update
  527.6 111.1 %reduce-scatter.5.cloned.1.call-done = f32[512,256]{1,0:T(8,128)} async-done(((f32[512,4096]{1,0:T(8,128)}), f32[512,256]{1,0:T(8,128)}) %reduce-scatter.5.cloned.1.call-update) | async-done | bytes 524304 | tf_op jit(solution)/shard_map/reduce_scatter | solution.py:50
Async XLA Ops:
  7.2 104.1 %all-gather.7.cloned.1.call-start = ((), (), s32[]{:S(2)}) async-start(), calls=%async_computation.3 | async-start | bytes 4456448 | tf_op jit(solution)/shard_map/all_gather | solution.py:16
  7.9 182.4 %all-gather.5.cloned.1.call-start = ((), (), s32[]{:S(2)}) async-start(), calls=%async_computation.2 | async-start | bytes 8912896 | tf_op jit(solution)/shard_map/all_gather | solution.py:42
  8.6 255.1 %all-gather.11.cloned.1.call-start = ((), (), s32[]{:S(2)}) async-start(), calls=%async_computation.5 | async-start | bytes 2228224 | tf_op jit(solution)/shard_map/all_gather | solution.py:17
  9.4 319.6 %copy-start.4 = (f32[512,256]{1,0:T(8,128)S(1)}, f32[512,256]{1,0:T(8,128)}, u32[]{:S(2)}) copy-start(f32[512,256]{1,0:T(8,128)} %param.8) | copy-start | bytes 1572868
  9.4 319.6 %copy-start.5 = (f32[512,256]{1,0:T(8,128)S(1)}, f32[512,256]{1,0:T(8,128)}, u32[]{:S(2)}) copy-start(f32[512,256]{1,0:T(8,128)} %param.9) | copy-start | bytes 1572868
  9.4 319.6 %all-gather.9.cloned.1.call-start = ((), (), s32[]{:S(2)}) async-start(), calls=%async_computation.4 | async-start | bytes 4456448 | tf_op jit(solution)/shard_map/all_gather | solution.py:30
  197.9 324.0 %reduce-scatter.3.cloned.1.call-start = ((), (), s32[]{:S(2)}) async-start(), calls=%async_computation.6 | async-start | bytes 8912896 | tf_op jit(solution)/shard_map/reduce_scatter | solution.py:46
  329.0 5.2 copy-start
  333.3 6.9 %copy-start.2 = (f32[512,256]{1,0:T(8,128)}, f32[512,256]{1,0:T(8,128)S(1)}, u32[]{:S(2)}) copy-start(f32[512,256]{1,0:T(8,128)S(1)} %get-tuple-element.3) | copy-start | bytes 1572868
  333.3 6.9 %copy-start.3 = (f32[512,256]{1,0:T(8,128)}, f32[512,256]{1,0:T(8,128)S(1)}, u32[]{:S(2)}) copy-start(f32[512,256]{1,0:T(8,128)S(1)} %get-tuple-element.4) | copy-start | bytes 1572868
  340.2 181.8 %copy-start.1 = (bf16[4096,256]{1,0:T(8,128)(2,1)S(1)}, bf16[4096,256]{1,0:T(8,128)(2,1)}, u32[]{:S(2)}) copy-start(bf16[4096,256]{1,0:T(8,128)(2,1)} %all-gather.11.cloned.1.call-done) | copy-start | bytes 6291460
  340.2 298.5 %reduce-scatter.5.cloned.1.call-start = ((), (), s32[]{:S(2)}) async-start(), calls=%async_computation.7 | async-start | bytes 8912896 | tf_op jit(solution)/shard_map/reduce_scatter | solution.py:50
Sparse Core Ops, SparseCore 0:
  9.8 101.4 all-gather.6
  113.9 76.2 all-gather.4
  192.1 71.6 all-gather.10
  266.7 62.2 all-gather.8
  340.3 181.6 reduce-scatter.2
  527.7 110.9 reduce-scatter.4
where the time goes:
time: 647 us; the launch traced here: 646 us
  waiting for transfers between devices  607 us (94%)
  matrix products  23.4 us (4%)
  between operations  14.2 us (2%)
    reduce_scatter x1, waiting for transfers between devices, shards(): back = lax.psum_scatter(whole, 'row', scatter_dimension=0, tiled=True)  182 us
    reduce_scatter x1, waiting for transfers between devices, shards(): update = lax.psum_scatter(spread, 'col', scatter_dimension=1, tiled=True)  111 us
    all_gather x1, waiting for transfers between devices, shards(): lax.all_gather(grad, 'row', axis=0, tiled=True)  102 us
    all_gather x1, waiting for transfers between devices, shards(): lax.all_gather(left_basis, 'col', axis=0, tiled=True)  79 us
    all_gather x1, waiting for transfers between devices, shards(): lax.all_gather(right_basis, 'row', axis=0, tiled=True)  65.8 us
    all_gather x1, waiting for transfers between devices, shards(): lax.all_gather(rotated, 'col', axis=1, tiled=True)  65.2 us
  transfers between devices with their start and end apart: 6, of which 6 were waited for; matrix products, arithmetic and copies ran while one was open for 1% of the time, Pallas kernels for 0%

commit v1 on v0

v1 whole, which is shorter than its diff:
```python
import functools

import jax
import jax.numpy as jnp
from jax import lax
from jax.experimental import pallas as pl
from jax.experimental.pallas import tpu as pltpu
from jax.sharding import PartitionSpec as P

STEP = 10
beta_first = 0.95
beta_second = 0.95
epsilon = 1e-08

MESH = pl.DeviceIdType.MESH
F32 = jnp.float32
BF16 = jnp.bfloat16

COPIES = 96


def dot(a, b, dims):
    return lax.dot_general(a, b, (dims, ((), ())), preferred_element_type=F32)


NN = ((1,), (0,))
TN = ((0,), (0,))
NT = ((1,), (1,))


def kernel(
    g_ref, l_ref, r_ref, avg_ref, sq_ref,
    update_ref, new_avg_ref, new_sq_ref,
    gbuf, lbuf, rbuf, rot, part, part_in, proj, proj_in, dbuf,
    wsend, wrecv, hilo, ssend, srecv, tsend, trecv,
    ssem, rsem, lsem,
):
    row, col = lax.axis_index("row"), lax.axis_index("col")
    z, h = row // 2, row % 2
    x, t, j = col // 4, (col // 2) % 2, col % 2
    matched = h == j
    half = 256
    lo, hi = pl.ds(0, half), pl.ds(half, half)

    def zq(d):
        return (z + d + 8) % 8

    def xq(d, other):
        return 2 * ((x + d + 4) % 4) + (1 - t if other else t)

    zp, zm = (2 * zq(1) + h, col), (2 * zq(-1) + h, col)
    xp, xm = (row, (col + 4) % 16), (row, (col + 12) % 16)
    yh = (row, 4 * x + 2 * (1 - t) + j)
    yl = (2 * z + 1 - h, col)
    core = (row, 4 * x + 2 * t + 1 - j)
    diag = (2 * z + 1 - h, 4 * x + 2 * t + 1 - j)

    barrier = pltpu.get_barrier_semaphore()
    for who in (zp, zm, xp, xm, yh, yl, core, diag):
        pl.semaphore_signal(barrier, inc=1, device_id=who, device_id_type=MESH)
    pl.semaphore_wait(barrier, 8)

    count = [0]
    sent = []

    def make(src, dst, who, slot=None):
        if slot is None:
            slot = count[0]
            count[0] += 1
        return pltpu.make_async_remote_copy(
            src_ref=src, dst_ref=dst, send_sem=ssem.at[slot], recv_sem=rsem.at[slot],
            device_id=who, device_id_type=MESH,
        )

    def push(src, dst, who):
        copy = make(src, dst, who)
        copy.start()
        sent.append(copy)
        return copy

    def same(ref, who):
        return push(ref, ref, who)

    own_g = pltpu.make_async_copy(g_ref, gbuf.at[z], lsem.at[0])
    own_g.start()
    swap = make(l_ref, lbuf.at[1 - j, xq(0, False)], diag)
    own_l = pltpu.make_async_copy(l_ref, lbuf.at[j, xq(0, False)], lsem.at[1])

    @pl.when(matched)
    def _():
        own_l.start()

    @pl.when(jnp.logical_not(matched))
    def _():
        swap.start()

    base_r = count[0]
    count[0] += 3
    r_far = make(r_ref, rbuf.at[z, j], (2 * z + 1 - h, 4 * x + 2 * t + h), base_r + j)
    r_near = make(r_ref, rbuf.at[z, j], core, base_r + 2)
    r_own = pltpu.make_async_copy(r_ref, rbuf.at[z, j], lsem.at[2])
    r_far.start()

    @pl.when(matched)
    def _():
        r_own.start()
        own_l.wait()

    @pl.when(jnp.logical_not(matched))
    def _():
        r_near.start()

    own_g.wait()

    class RingZ:
        def __init__(self, buf, cut):
            self.buf, self.cut = buf, cut

        def start(self):
            self.p, self.m = same(self.buf.at[z], zp), same(self.buf.at[z], zm)

        def step(self, k):
            self.p.wait_recv()
            down = self.buf.at[zq(-k)]
            self.p = same(down if k < 3 else self.cut(down, 0), zp)
            self.m.wait_recv()
            up = self.buf.at[zq(k)]
            self.m = same(up if k < 3 else self.cut(up, 1), zm)

        def finish(self):
            self.p.wait_recv()
            self.m.wait_recv()

    class RingX:
        def __init__(self, buf, share):
            self.buf, self.share = buf, share
            self.p, self.m = {}, {}

        def go(self, other):
            block = self.buf.at[xq(0, other)]
            if not other:
                self.y = same(block, yh)
            self.p[other], self.m[other] = same(block, xp), same(block, xm)
            self.share(xq(0, other))

        def second(self):
            self.y.wait_recv()
            self.go(True)

        def forward(self, other):
            self.p[other].wait_recv()
            q = xq(-1, other)
            self.p[other] = same(self.buf.at[q, lo], xp)
            self.share(q)
            self.m[other].wait_recv()
            q = xq(1, other)
            self.m[other] = same(self.buf.at[q, hi], xm)
            self.share(q)

        def finish(self, other):
            self.p[other].wait_recv()
            self.m[other].wait_recv()
            self.share(xq(2, other))

    shared = []

    def share_left(q):
        shared.append(same(lbuf.at[j, q], core))

    rows_cut = lambda ref, k: ref.at[lo if k == 0 else hi]
    ring_g = RingZ(gbuf, rows_cut)
    ring_r = RingZ(rbuf, lambda ref, k: ref.at[k])
    ring_l = RingX(lbuf.at[j], share_left)

    ring_g.start()

    @pl.when(jnp.logical_not(matched))
    def _():
        swap.wait_recv()

    ring_l.go(False)
    ring_g.step(1)

    @pl.when(matched)
    def _():
        make(r_ref, rbuf.at[z, 1 - j], core, base_r + 2).wait_recv()
        r_own.wait()

    @pl.when(jnp.logical_not(matched))
    def _():
        make(r_ref, rbuf.at[z, 0], core, base_r).wait_recv()
        make(r_ref, rbuf.at[z, 1], core, base_r + 1).wait_recv()

    ring_l.second()
    ring_g.step(2)
    ring_r.start()
    ring_l.forward(False)
    ring_g.step(3)
    ring_r.step(1)
    ring_l.forward(True)
    ring_g.finish()
    ring_r.step(2)

    part[...] = jnp.zeros_like(part)

    def rotate(q):
        for i in range(2):
            part[i] += dot(lbuf[i, q], gbuf[q], TN)

    for copy in shared[:6]:
        copy.wait_recv()

    def near(n, carry):
        q = 2 * ((x + n // 2 + 3) % 4) + n % 2
        rotate(q)
        return carry

    lax.fori_loop(0, 6, near, 0)
    ring_l.finish(False)
    ring_l.finish(True)
    for copy in shared[6:]:
        copy.wait_recv()

    def far(n, carry):
        rotate(2 * ((x + 2) % 4) + n)
        return carry

    lax.fori_loop(0, 2, far, 0)
    exchange = push(part.at[1 - h], part_in, yl)
    ring_r.step(3)
    exchange.wait_recv()
    rot[xq(0, False)] = (part[h] + part_in[...]).astype(BF16)

    ring_rot = RingX(rot, lambda q: None)
    ring_rot.go(False)
    ring_r.finish()
    ring_rot.second()
    ring_rot.forward(False)
    ring_rot.forward(True)

    proj[...] = jnp.zeros_like(proj)

    def project(q):
        for c in range(2):
            proj[c] += dot(rot[q], rbuf[q, c], NN)

    def near_p(n, carry):
        project(2 * ((x + n // 2 + 3) % 4) + n % 2)
        return carry

    lax.fori_loop(0, 6, near_p, 0)
    ring_rot.finish(False)
    ring_rot.finish(True)

    def far_p(n, carry):
        project(2 * ((x + 2) % 4) + n)
        return carry

    lax.fori_loop(0, 2, far_p, 0)
    cross = push(proj.at[1 - j], proj_in, core)
    cross.wait_recv()
    projected = proj[j] + proj_in[...]
    new_avg = beta_first * avg_ref[...] + (1.0 - beta_first) * projected
    new_sq = beta_second * sq_ref[...] + (1.0 - beta_second) * projected * projected
    new_avg_ref[...] = new_avg
    new_sq_ref[...] = new_sq
    first_fix = 1.0 - beta_first**STEP
    second_fix = 1.0 - beta_second**STEP
    dbuf[h] = (new_avg / first_fix / (jnp.sqrt(new_sq / second_fix) + epsilon)).astype(BF16)
    push(dbuf.at[h], dbuf.at[h], yl).wait_recv()

    def spread_left(q, rows):
        return dot(lbuf[0, q, rows], dbuf[0], NN) + dot(lbuf[1, q, rows], dbuf[1], NN)

    both = ((lo, 0), (hi, 1))
    flying = {}
    for s in range(1, 5):
        for way, who, first in ((0, zp, 0), (1, zm, 1)):
            q = zq(5 - s if way == 0 else s - 5)
            for rows, k in (both[1 - first], both[first]):
                if s == 1 and k != first:
                    continue
                value = spread_left(q, rows)
                before = flying.get((way, s - 1, k))
                if before is not None:
                    before.wait_recv()
                    value += wrecv[way, s - 2, rows].astype(F32)
                wsend[way, s - 1, rows] = value.astype(BF16)
                flying[way, s, k] = push(
                    wsend.at[way, s - 1, rows], wrecv.at[way, s - 1, rows], who
                )
    for rows, k in both:
        value = spread_left(z, rows)
        for way in range(2):
            flying[way, 4, k].wait_recv()
            value += wrecv[way, 3, rows].astype(F32)
        high = value.astype(BF16)
        hilo[j, 0, rows] = high
        hilo[j, 1, rows] = (value - high.astype(F32)).astype(BF16)
    push(hilo.at[j], hilo.at[j], core).wait_recv()

    def spread_right(q, rows):
        total = dot(hilo[0, 0, rows], rbuf[q, 0], NT)
        total += dot(hilo[1, 0, rows], rbuf[q, 1], NT)
        total += dot(hilo[0, 1, rows], rbuf[q, 0], NT)
        total += dot(hilo[1, 1, rows], rbuf[q, 1], NT)
        return total

    going = {}

    def send(o, way, s, rows, k, value):
        ssend[o, way, s, rows] = value.astype(BF16)
        going[o, way, s, k] = push(
            ssend.at[o, way, s, rows], srecv.at[o, way, s, rows], (xp, xm)[way]
        )

    for o in (1, 0):
        for way in range(2):
            rows, k = both[way]
            send(o, way, 0, rows, k, spread_right(xq(2, o == 1), rows))
        for way in range(2):
            rows, k = both[1 - way]
            send(o, way, 1, rows, k, spread_right(xq(1 - 2 * way, o == 1), rows))
    for o in (1, 0):
        for way in range(2):
            rows, k = both[way]
            value = spread_right(xq(1 - 2 * way, o == 1), rows)
            going[o, way, 0, k].wait_recv()
            send(o, way, 1, rows, k, value + srecv[o, way, 0, rows].astype(F32))
    last = {}
    for o in (1, 0):
        for rows, k in both:
            value = spread_right(xq(0, o == 1), rows)
            for way in range(2):
                going[o, way, 1, k].wait_recv()
                value += srecv[o, way, 1, rows].astype(F32)
            if o == 1:
                tsend[rows] = value.astype(BF16)
                last[k] = push(tsend.at[rows], trecv.at[rows], yh)
            else:
                last[k].wait_recv()
                update_ref[rows] = value + trecv[rows].astype(F32)

    for copy in sent:
        copy.wait_send()
    r_far.wait_send()

    @pl.when(jnp.logical_not(matched))
    def _():
        swap.wait_send()
        r_near.wait_send()


def shards(grad, left_basis, right_basis, exp_avg, exp_avg_sq):
    block = jax.ShapeDtypeStruct((512, 256), F32)
    vmem = pl.BlockSpec(memory_space=pltpu.VMEM)
    return pl.pallas_call(
        kernel,
        out_shape=(block, block, block),
        in_specs=[vmem] * 5,
        out_specs=(vmem,) * 3,
        scratch_shapes=[
            pltpu.VMEM((8, 512, 256), BF16),
            pltpu.VMEM((2, 8, 512, 512), BF16),
            pltpu.VMEM((8, 2, 256, 256), BF16),
            pltpu.VMEM((8, 512, 256), BF16),
            pltpu.VMEM((2, 512, 256), F32),
            pltpu.VMEM((512, 256), F32),
            pltpu.VMEM((2, 512, 256), F32),
            pltpu.VMEM((512, 256), F32),
            pltpu.VMEM((2, 512, 256), BF16),
            pltpu.VMEM((2, 4, 512, 256), BF16),
            pltpu.VMEM((2, 4, 512, 256), BF16),
            pltpu.VMEM((2, 2, 512, 256), BF16),
            pltpu.VMEM((2, 2, 2, 512, 256), BF16),
            pltpu.VMEM((2, 2, 2, 512, 256), BF16),
            pltpu.VMEM((512, 256), BF16),
            pltpu.VMEM((512, 256), BF16),
            pltpu.SemaphoreType.DMA((COPIES,)),
            pltpu.SemaphoreType.DMA((COPIES,)),
            pltpu.SemaphoreType.DMA((3,)),
        ],
        compiler_params=pltpu.CompilerParams(
            collective_id=0, has_side_effects=True, vmem_limit_bytes=56 * 1024 * 1024
        ),
        cost_estimate=pl.CostEstimate(flops=6_500_000_000, bytes_accessed=4_000_000, transcendentals=0),
    )(grad, left_basis, right_basis, exp_avg, exp_avg_sq)


def solution(mesh):
    return jax.shard_map(
        shards,
        mesh=mesh,
        in_specs=(
            P("row", "col"),
            P("col", "row"),
            P("row", "col"),
            P("row", "col"),
            P("row", "col"),
        ),
        out_specs=(P("row", "col"), P("row", "col"), P("row", "col")),
        check_vma=False,
    )
```

time: 647 us -> 159 us (0.25)
  the two profiles are of different devices: /device:TPU:10 before, /device:TPU:25 now
where the time goes in v1:
time: 159 us
  Pallas kernels  154 us (97%)
  local copies, waits for them, and re-layouts  3.95 us (2%)
    pallas_call x1, Pallas kernels, shards(): pl.pallas_call(kernel, out_shape=(block, block, block), in_specs=[vmem] *...  154 us
    unnamed x7, local copies, waits for them, and re-layouts  3.95 us

profile of v1, /device:TPU:25, one launch (start us, length us, event | category | flops | bytes accessed | tf_op | source)
XLA Modules:
  0.0 158.6 jit_solution(12610017057703064340)
XLA Ops:
  0.6 154.0 %shard_map.76 = (f32[512,256]{1,0:T(8,128)}, f32[512,256]{1,0:T(8,128)}, f32[512,256]{1,0:T(8,128)}) custom-call(bf16[512,256]{1,0:T(8,128)(2,1)} %g_ref.1, bf16[512,512]{1,0:T(8,128)(2,1)} %l_ref.1, bf16[256,256]{1,0:T(8,128)(2,1)} %r_ref.1, f32[512,256]{1,0:T(8,128)} %avg_ref.1, f32[512,256]{1,0:T(8,128)} %sq_ref.1), custom_call_target="tpu_custom_call" | custom-call | flops 6499999744 | bytes 4000000 | tf_op jit(solution)/shard_map/pallas_call | solution.py:357
  154.6 0.0 copy-start.1
  154.6 1.9 %copy.11 = f32[512,256]{1,0:T(8,128)} copy(f32[512,256]{1,0:T(8,128)} %get-tuple-element.6) | data formatting | bytes 1048576
  156.6 0.0 copy-done.1
  156.6 0.0 copy-start
  156.6 0.8 copy.12
  157.4 0.4 copy-done
  157.8 0.8 copy.13
Async XLA Ops:
  154.6 1.9 %copy-start.1 = (f32[512,256]{1,0:T(8,128)S(1)}, f32[512,256]{1,0:T(8,128)}, u32[]{:S(2)}) copy-start(f32[512,256]{1,0:T(8,128)} %get-tuple-element.7) | copy-start | bytes 1572868
  156.6 1.2 copy-start

commit v2 on v0

v2 whole, which is shorter than its diff:
```python
import functools

import jax
import jax.numpy as jnp
from jax import lax
from jax.experimental import pallas as pl
from jax.experimental.pallas import tpu as pltpu
from jax.sharding import PartitionSpec as P

STEP = 10
beta_first = 0.95
beta_second = 0.95
epsilon = 1e-08

MESH = pl.DeviceIdType.MESH
F32 = jnp.float32
BF16 = jnp.bfloat16

COPIES = 160


def dot(a, b, dims):
    return lax.dot_general(a, b, (dims, ((), ())), preferred_element_type=F32)


NN = ((1,), (0,))
TN = ((0,), (0,))
NT = ((1,), (1,))


def kernel(
    g_ref, l_ref, r_ref, avg_in, sq_in,
    update_out, avg_out, sq_out,
    update, avg, sq,
    gbuf, lbuf, rbuf, rot, part, part_in, proj, proj_in, dbuf,
    whole, wsend, wrecv, hilo, ssend, srecv, keep, tsend, trecv,
    ssem, rsem, lsem,
):
    row, col = lax.axis_index("row"), lax.axis_index("col")
    z, h = row // 2, row % 2
    x, t, j = col // 4, (col // 2) % 2, col % 2
    matched = h == j
    half = 256
    lo, hi = pl.ds(0, half), pl.ds(half, half)

    def zq(d):
        return (z + d + 8) % 8

    def xq(d, other):
        return 2 * ((x + d + 4) % 4) + (1 - t if other else t)

    zp, zm = (2 * zq(1) + h, col), (2 * zq(-1) + h, col)
    xp, xm = (row, (col + 4) % 16), (row, (col + 12) % 16)
    yh = (row, 4 * x + 2 * (1 - t) + j)
    yl = (2 * z + 1 - h, col)
    core = (row, 4 * x + 2 * t + 1 - j)
    diag = (2 * z + 1 - h, 4 * x + 2 * t + 1 - j)

    count = [0]
    sent = []

    def make(src, dst, who, slot=None):
        if slot is None:
            slot = count[0]
            count[0] += 1
        return pltpu.make_async_remote_copy(
            src_ref=src, dst_ref=dst, send_sem=ssem.at[slot], recv_sem=rsem.at[slot],
            device_id=who, device_id_type=MESH,
        )

    def push(src, dst, who):
        copy = make(src, dst, who)
        copy.start()
        sent.append(copy)
        return copy

    def later(src, dst, who):
        copy = make(src, dst, who)
        sent.append(copy)
        return copy

    def same(ref, who):
        return push(ref, ref, who)

    halves = ((0, 256), (256, 256))

    first = xq(0, False)
    own_g = pltpu.make_async_copy(g_ref, gbuf.at[z], lsem.at[0])
    own_l = pltpu.make_async_copy(l_ref, lbuf.at[j, first], lsem.at[1])
    r_own = pltpu.make_async_copy(r_ref, rbuf.at[z, j], lsem.at[2])
    swaps = [
        make(l_ref.at[pl.ds(*r)], lbuf.at[1 - j, first, pl.ds(*r)], diag) for r in halves
    ]

    keep_avg = pltpu.make_async_copy(avg_in, avg, lsem.at[3])
    keep_sq = pltpu.make_async_copy(sq_in, sq, lsem.at[4])
    own_g.start()
    keep_avg.start()
    keep_sq.start()

    @pl.when(matched)
    def _():
        own_l.start()
        r_own.start()

    barrier = pltpu.get_barrier_semaphore()
    for who in (zp, zm, xp, xm, yh, yl, core, diag):
        pl.semaphore_signal(barrier, inc=1, device_id=who, device_id_type=MESH)
    pl.semaphore_wait(barrier, 8)

    @pl.when(jnp.logical_not(matched))
    def _():
        for copy in swaps:
            copy.start()

    base_r = count[0]
    count[0] += 3
    r_far = make(r_ref, rbuf.at[z, j], (2 * z + 1 - h, 4 * x + 2 * t + h), base_r + j)
    r_near = make(r_ref, rbuf.at[z, j], core, base_r + 2)

    def drain():
        for copy in sent:
            copy.wait_send()
        r_far.wait_send()

        @pl.when(jnp.logical_not(matched))
        def _():
            for copy in swaps:
                copy.wait_send()
            r_near.wait_send()

    class RingZ:
        def __init__(self, buf, cut):
            def both(k, low, high):
                return later(low, low, zp), later(high, high, zm)

            self.steps = [both(0, buf.at[z], buf.at[z])]
            for k in (1, 2, 3):
                low, high = buf.at[zq(-k)], buf.at[zq(k)]
                if k == 3:
                    low, high = cut(low, 0), cut(high, 1)
                self.steps.append(both(k, low, high))

        def start(self):
            for copy in self.steps[0]:
                copy.start()

        def step(self, k):
            for before, copy in zip(self.steps[k - 1], self.steps[k]):
                before.wait_recv()
                copy.start()

        def finish(self):
            for copy in self.steps[3]:
                copy.wait_recv()

    class RingX:
        def __init__(self, buf, top, size):
            low, high = pl.ds(top, size // 2), pl.ds(top + size // 2, size // 2)

            def to(q, rows, who):
                return later(buf.at[q, rows], buf.at[q, rows], who)

            self.y = to(xq(0, False), pl.ds(top, size), yh)
            self.lead, self.rest, self.passed = {}, {}, {}
            for other in (False, True):
                q = xq(0, other)
                self.lead[other] = to(q, low, xp), to(q, high, xm)
                self.rest[other] = to(q, high, xp), to(q, low, xm)
                self.passed[other] = to(xq(-1, other), low, xp), to(xq(1, other), high, xm)

        def go(self, other):
            if not other:
                self.y.start()
            for copy in self.lead[other] + self.rest[other]:
                copy.start()

        def second(self):
            self.y.wait_recv()
            self.go(True)

        def forward(self, other):
            for before, copy in zip(self.lead[other], self.passed[other]):
                before.wait_recv()
                copy.start()

        def complete(self, other):
            for copy in self.rest[other]:
                copy.wait_recv()

        def finish(self, other):
            for copy in self.passed[other]:
                copy.wait_recv()

    ring_g = RingZ(gbuf, lambda ref, k: ref.at[lo if k == 0 else hi])
    ring_r = RingZ(rbuf, lambda ref, k: ref.at[k])
    ring_l = [RingX(lbuf.at[j], *r) for r in halves]

    order = [(0, False), (-1, False), (1, False), (2, False), (0, True), (-1, True), (1, True), (2, True)]
    shared = [later(lbuf.at[j, xq(*o)], lbuf.at[j, xq(*o)], core) for o in order]

    def share(*which):
        for n in which:
            shared[n].start()

    def take(*which):
        for n in which:
            shared[n].wait_recv()

    def left(event, *which):
        for ring in ring_l:
            getattr(ring, event)(*which)

    def rotate(i, first, number):
        def body(n, carry):
            q = 2 * ((x + n // 2 + first) % 4) + n % 2
            part[i] += dot(lbuf[i, q], gbuf[q], TN)
            return carry

        lax.fori_loop(0, number, body, 0)

    pieces = tuple((128 * n, 128) for n in range(4))
    exchange = [later(part.at[1 - h, pl.ds(*r)], part_in.at[pl.ds(*r)], yl) for r in pieces]

    def give():
        for copy in exchange:
            copy.start()

    part[...] = jnp.zeros_like(part)

    @pl.when(matched)
    def _():
        own_l.wait()
        left("go", False)
        share(0)
        r_far.start()
        own_g.wait()
        ring_g.start()
        left("forward", False)
        ring_g.step(1)
        left("complete", False)
        share(1, 2)
        ring_g.step(2)
        left("finish", False)
        share(3)
        ring_g.step(3)
        make(r_ref, rbuf.at[z, 1 - j], core, base_r + 2).wait_recv()
        r_own.wait()
        ring_r.start()
        take(0, 1, 2, 4, 5, 6)
        left("second")
        share(4)
        ring_g.finish()
        rotate(1 - h, 3, 6)
        left("forward", True)
        ring_r.step(1)
        take(3, 7)
        rotate(1 - h, 2, 2)
        give()
        left("complete", True)
        share(5, 6)
        ring_r.step(2)
        rotate(h, 3, 6)
        left("finish", True)
        share(7)
        rotate(h, 2, 2)

    @pl.when(jnp.logical_not(matched))
    def _():
        own_g.wait()
        ring_g.start()
        for ring, copy in zip(ring_l, swaps):
            copy.wait_recv()
            ring.go(False)
        share(0)
        r_far.start()
        r_near.start()
        ring_g.step(1)
        left("forward", False)
        left("second")
        share(4)
        left("complete", False)
        share(1, 2)
        ring_g.step(2)
        left("forward", True)
        left("finish", False)
        share(3)
        ring_g.step(3)
        left("complete", True)
        share(5, 6)
        make(r_ref, rbuf.at[z, 0], core, base_r).wait_recv()
        make(r_ref, rbuf.at[z, 1], core, base_r + 1).wait_recv()
        ring_r.start()
        left("finish", True)
        share(7)
        ring_g.finish()
        rotate(1 - h, 0, 8)
        give()
        ring_r.step(1)
        take(0, 1, 2, 4, 5, 6)
        rotate(h, 3, 6)
        ring_r.step(2)
        take(3, 7)
        rotate(h, 2, 2)


    ring_rot = [RingX(rot, *r) for r in halves]
    for n, r in enumerate(halves):
        exchange[2 * n].wait_recv()
        exchange[2 * n + 1].wait_recv()
        rows = pl.ds(*r)
        rot[first, rows] = (part[h, rows] + part_in[rows]).astype(BF16)
        ring_rot[n].go(False)
    ring_r.step(3)
    ring_rot[0].second()
    ring_rot[0].forward(False)
    ring_rot[1].second()
    ring_rot[0].forward(True)
    ring_rot[1].forward(False)
    ring_rot[1].forward(True)
    for other in (False, True):
        ring_rot[0].complete(other)
        ring_rot[0].finish(other)
    ring_r.finish()

    keep_avg.wait()
    keep_sq.wait()
    first_fix = 1.0 - beta_first**STEP
    second_fix = 1.0 - beta_second**STEP
    give_d = []
    for n, r in enumerate(halves):
        rows = pl.ds(*r)
        if n == 1:
            for other in (False, True):
                ring_rot[1].complete(other)
                ring_rot[1].finish(other)
        proj[:, rows] = jnp.zeros((2, 256, 256), F32)

        def project(q, carry):
            for c in range(2):
                proj[c, rows] += dot(rot[q, rows], rbuf[q, c], NN)
            return carry

        lax.fori_loop(0, 8, project, 0)
        push(proj.at[1 - j, rows], proj_in.at[rows], core).wait_recv()
        projected = proj[j, rows] + proj_in[rows]
        new_avg = beta_first * avg[rows] + (1.0 - beta_first) * projected
        new_sq = beta_second * sq[rows] + (1.0 - beta_second) * projected * projected
        avg[rows] = new_avg
        sq[rows] = new_sq
        dbuf[h, rows] = (
            new_avg / first_fix / (jnp.sqrt(new_sq / second_fix) + epsilon)
        ).astype(BF16)
        give_d.append(same(dbuf.at[h, rows], yl))
    out_avg = pltpu.make_async_copy(avg, avg_out, lsem.at[3])
    out_sq = pltpu.make_async_copy(sq, sq_out, lsem.at[4])
    out_avg.start()
    out_sq.start()
    for copy in give_d:
        copy.wait_recv()

    def quarters(n):
        return (pl.ds(256 * n, 128), pl.ds(256 * n + 128, 128))

    def spread_left(q):
        whole[q] = dot(lbuf[0, q], dbuf[0], NN) + dot(lbuf[1, q], dbuf[1], NN)

    flying = {}

    def back_send(n, s, way, k):
        rows = quarters(n)[k]
        value = whole[zq(5 - s if way == 0 else s - 5), rows]
        before = flying.get((n, way, s - 1, k))
        if before is not None:
            before.wait_recv()
            value += wrecv[way, s - 2, rows].astype(F32)
        wsend[way, s - 1, rows] = value.astype(BF16)
        flying[n, way, s, k] = push(
            wsend.at[way, s - 1, rows], wrecv.at[way, s - 1, rows], (zp, zm)[way]
        )

    def back_step(n, s):
        for k in (0, 1):
            for way in (0, 1):
                if s > 2 or k == 0:
                    back_send(n, s, way, (1 - way, way)[k] if s > 2 else way)

    def back_end(n):
        rows = pl.ds(256 * n, 256)
        value = whole[z, rows]
        for way in range(2):
            for k in range(2):
                flying[n, way, 4, k].wait_recv()
        for way in range(2):
            value += wrecv[way, 3, rows].astype(F32)
        high = value.astype(BF16)
        hilo[n, j, 0] = high
        hilo[n, j, 1] = (value - high.astype(F32)).astype(BF16)
        push(hilo.at[n, j], hilo.at[n, j], core).wait_recv()

    def spread_right(n, q):
        total = dot(hilo[n, 0].reshape(512, 256), rbuf[q, 0], NT)
        total += dot(hilo[n, 1].reshape(512, 256), rbuf[q, 1], NT)
        return total[:256] + total[256:]

    going, kept, last = {}, {}, {}

    def send(n, o, way, s, k, value):
        rows = quarters(n)[k]
        ssend[o, way, s, rows] = value.astype(BF16)
        going[n, o, way, s, k] = push(
            ssend.at[o, way, s, rows], srecv.at[o, way, s, rows], (xp, xm)[way]
        )

    def part_of(value, k):
        return value[128 * k : 128 * k + 128]

    def up_first(n):
        for o in (1, 0):
            value = spread_right(n, xq(2, o == 1))
            for way in range(2):
                send(n, o, way, 0, way, part_of(value, way))
        for o in (1, 0):
            for way in range(2):
                value = spread_right(n, xq(1 - 2 * way, o == 1))
                send(n, o, way, 1, 1 - way, part_of(value, 1 - way))
                keep[o, way, quarters(n)[way]] = part_of(value, way)

    def up_second(n):
        for o in (1, 0):
            for way in range(2):
                rows = quarters(n)[way]
                going[n, o, way, 0, way].wait_recv()
                send(n, o, way, 1, way, keep[o, way, rows] + srecv[o, way, 0, rows].astype(F32))

    def up_third(n, o):
        rows = pl.ds(256 * n, 256)
        value = spread_right(n, xq(0, o == 1))
        for way in range(2):
            for k in range(2):
                going[n, o, way, 1, k].wait_recv()
        for way in range(2):
            value += srecv[o, way, 1, rows].astype(F32)
        if o == 1:
            tsend[rows] = value.astype(BF16)
            last[n] = push(tsend.at[rows], trecv.at[rows], yh)
        else:
            last[n].wait_recv()
            update[rows] = value + trecv[rows].astype(F32)

    spread_left(zq(4))
    for n in range(2):
        for way in range(2):
            back_send(n, 1, way, way)
    spread_left(zq(3))
    spread_left(zq(-3))
    for n in range(2):
        for way in range(2):
            back_send(n, 2, way, 1 - way)
    spread_left(zq(2))
    spread_left(zq(-2))
    back_step(0, 2)
    spread_left(zq(1))
    spread_left(zq(-1))
    back_step(0, 3)
    back_step(1, 2)
    spread_left(z)
    back_step(0, 4)
    back_step(1, 3)
    back_step(1, 4)
    back_end(0)
    up_first(0)
    up_second(0)
    back_end(1)
    up_first(1)
    up_third(0, 1)
    up_second(1)
    up_third(0, 0)
    up_third(1, 1)
    up_third(1, 0)
    out_update = pltpu.make_async_copy(update, update_out, lsem.at[5])
    out_update.start()
    drain()
    out_avg.wait()
    out_sq.wait()
    out_update.wait()


def shards(grad, left_basis, right_basis, exp_avg, exp_avg_sq):
    block = jax.ShapeDtypeStruct((512, 256), F32)
    place = pl.BlockSpec(memory_space=pl.ANY)
    return pl.pallas_call(
        kernel,
        out_shape=(block, block, block),
        in_specs=[place] * 5,
        out_specs=(place,) * 3,
        scratch_shapes=[
            pltpu.VMEM((512, 256), F32),
            pltpu.VMEM((512, 256), F32),
            pltpu.VMEM((512, 256), F32),
            pltpu.VMEM((8, 512, 256), BF16),
            pltpu.VMEM((2, 8, 512, 512), BF16),
            pltpu.VMEM((8, 2, 256, 256), BF16),
            pltpu.VMEM((8, 512, 256), BF16),
            pltpu.VMEM((2, 512, 256), F32),
            pltpu.VMEM((512, 256), F32),
            pltpu.VMEM((2, 512, 256), F32),
            pltpu.VMEM((512, 256), F32),
            pltpu.VMEM((2, 512, 256), BF16),
            pltpu.VMEM((8, 512, 256), F32),
            pltpu.VMEM((2, 4, 512, 256), BF16),
            pltpu.VMEM((2, 4, 512, 256), BF16),
            pltpu.VMEM((2, 2, 2, 256, 256), BF16),
            pltpu.VMEM((2, 2, 2, 512, 256), BF16),
            pltpu.VMEM((2, 2, 2, 512, 256), BF16),
            pltpu.VMEM((2, 2, 512, 256), F32),
            pltpu.VMEM((512, 256), BF16),
            pltpu.VMEM((512, 256), BF16),
            pltpu.SemaphoreType.DMA((COPIES,)),
            pltpu.SemaphoreType.DMA((COPIES,)),
            pltpu.SemaphoreType.DMA((6,)),
        ],
        compiler_params=pltpu.CompilerParams(
            collective_id=0, has_side_effects=True, vmem_limit_bytes=56 * 1024 * 1024
        ),
        cost_estimate=pl.CostEstimate(flops=6_500_000_000, bytes_accessed=4_000_000, transcendentals=0),
    )(grad, left_basis, right_basis, exp_avg, exp_avg_sq)


def solution(mesh):
    return jax.shard_map(
        shards,
        mesh=mesh,
        in_specs=(
            P("row", "col"),
            P("col", "row"),
            P("row", "col"),
            P("row", "col"),
            P("row", "col"),
        ),
        out_specs=(P("row", "col"), P("row", "col"), P("row", "col")),
        check_vma=False,
    )
```

time: 647 us -> 138 us (0.21)
  waiting for transfers between devices: 607 us -> 0 us
  Pallas kernels: 0 us -> 131 us
  matrix products: 23.4 us -> 0 us
  between operations: 14.2 us -> 0.65 us
    all_gather x4 -> x0, waiting for transfers between devices: 312 us -> none  [the longest x1 102 us: shards(): lax.all_gather(grad, 'row', axis=0, tiled=True)]
    reduce_scatter x2 -> x0, waiting for transfers between devices: 293 us -> none  [the longest x1 182 us: shards(): back = lax.psum_scatter(whole, 'row', scatter_dimension=0, tiled=True)]
    pallas_call x0 -> x1, Pallas kernels: none -> 131 us  [shards(): pl.pallas_call(kernel, out_shape=(block, block, block), in_specs=[place]...]
    dot_general x4 -> x0, matrix products: 23.4 us -> none  [the longest x1 7.65 us: shards(): lax.dot_general(lax.all_gather(left_basis, 'col', axis=0, tiled=True), wi...]
  transfers between devices with their start and end apart: 6 -> 0, of which waited for: 6 -> 0; matrix products, arithmetic and copies ran while one was open for 1% -> 0% of each run, Pallas kernels for 0% -> 0%
where the time goes in v2:
time: 138 us; the launch traced here: 136 us
  Pallas kernels  131 us (95%)
  local copies, waits for them, and re-layouts  3.95 us (3%)
    pallas_call x1, Pallas kernels, shards(): pl.pallas_call(kernel, out_shape=(block, block, block), in_specs=[place]...  131 us
    unnamed x7, local copies, waits for them, and re-layouts  3.95 us

profile of v2, /device:TPU:10, one launch (start us, length us, event | category | flops | bytes accessed | tf_op | source)
XLA Modules:
  0.0 135.9 jit_solution(1287585266826055592)
XLA Ops:
  0.6 131.3 %shard_map.76 = (f32[512,256]{1,0:T(8,128)}, f32[512,256]{1,0:T(8,128)}, f32[512,256]{1,0:T(8,128)}) custom-call(bf16[512,256]{1,0:T(8,128)(2,1)} %g_ref.1, bf16[512,512]{1,0:T(8,128)(2,1)} %l_ref.1, bf16[256,256]{1,0:T(8,128)(2,1)} %r_ref.1, f32[512,256]{1,0:T(8,128)} %avg_in.1, f32[512,256]{1,0:T(8,128)} %sq_in.1), custom_call_target="tpu_custom_call" | custom-call | flops 6499999744 | bytes 4000000 | tf_op jit(solution)/shard_map/pallas_call | solution.py:492
  131.9 0.0 copy-start.1
  131.9 1.9 %copy.11 = f32[512,256]{1,0:T(8,128)} copy(f32[512,256]{1,0:T(8,128)} %get-tuple-element.6) | data formatting | bytes 1048576
  133.8 0.0 copy-done.1
  133.8 0.0 copy-start
  133.8 0.8 copy.12
  134.6 0.4 copy-done
  135.1 0.8 copy.13
Async XLA Ops:
  131.9 1.9 %copy-start.1 = (f32[512,256]{1,0:T(8,128)S(1)}, f32[512,256]{1,0:T(8,128)}, u32[]{:S(2)}) copy-start(f32[512,256]{1,0:T(8,128)} %get-tuple-element.7) | copy-start | bytes 1572868
  133.8 1.2 copy-start

commit v3 on v2

--- a/solution.py
+++ b/solution.py
@@ -30,10 +30,10 @@
 
 def kernel(
     g_ref, l_ref, r_ref, avg_in, sq_in,
-    update_out, avg_out, sq_out,
+    near_out, far_out, proj_out,
     update, avg, sq,
     gbuf, lbuf, rbuf, rot, part, part_in, proj, proj_in, dbuf,
-    whole, wsend, wrecv, hilo, ssend, srecv, keep, tsend, trecv,
+    whole, wsend, wrecv, hilo, ssend, srecv, keep, opposite, tsend, trecv,
     ssem, rsem, lsem,
 ):
     row, col = lax.axis_index("row"), lax.axis_index("col")
@@ -122,9 +122,19 @@
         for copy in sent:
             copy.wait_send()
         r_far.wait_send()
+        for ring in ring_rot:
+            ring.far[0].wait_send()
+
+        @pl.when(matched)
+        def _():
+            for ring in ring_l:
+                ring.far[0].wait_send()
 
         @pl.when(jnp.logical_not(matched))
         def _():
+            for ring in ring_l:
+                for copy in ring.ring:
+                    copy.wait_send()
             for copy in swaps:
                 copy.wait_send()
             r_near.wait_send()
@@ -162,16 +172,24 @@
                 return later(buf.at[q, rows], buf.at[q, rows], who)
 
             self.y = to(xq(0, False), pl.ds(top, size), yh)
-            self.lead, self.rest, self.passed = {}, {}, {}
+            self.lead, self.rest = {}, {}
             for other in (False, True):
                 q = xq(0, other)
                 self.lead[other] = to(q, low, xp), to(q, high, xm)
                 self.rest[other] = to(q, high, xp), to(q, low, xm)
-                self.passed[other] = to(xq(-1, other), low, xp), to(xq(1, other), high, xm)
+            self.passed = to(xq(-1, False), low, xp), to(xq(1, False), high, xm)
+            down, up, far = xq(-1, True), xq(1, True), xq(2, False)
+            whole_block = buf.at[far, pl.ds(top, size)]
+            self.ring = (
+                make(buf.at[down, low], buf.at[down, low], xp),
+                make(buf.at[up, high], buf.at[up, high], xm),
+            )
+            self.far = (make(whole_block, whole_block, yh),)
+
+        def across(self):
+            self.y.start()
 
         def go(self, other):
-            if not other:
-                self.y.start()
             for copy in self.lead[other] + self.rest[other]:
                 copy.start()
 
@@ -179,17 +197,28 @@
             self.y.wait_recv()
             self.go(True)
 
-        def forward(self, other):
-            for before, copy in zip(self.lead[other], self.passed[other]):
+        def forward(self):
+            for before, copy in zip(self.lead[False], self.passed):
                 before.wait_recv()
                 copy.start()
 
-        def complete(self, other):
-            for copy in self.rest[other]:
+        def forward_ring(self):
+            for before, copy in zip(self.lead[True], self.ring):
+                before.wait_recv()
+                copy.start()
+
+        def forward_far(self):
+            for copy in self.passed:
                 copy.wait_recv()
-
-        def finish(self, other):
-            for copy in self.passed[other]:
+            self.far[0].start()
+
+        def complete(self, *others):
+            for other in others:
+                for copy in self.rest[other]:
+                    copy.wait_recv()
+
+        def finish_far(self):
+            for copy in self.lead[True] + self.rest[True] + self.far:
                 copy.wait_recv()
 
     ring_g = RingZ(gbuf, lambda ref, k: ref.at[lo if k == 0 else hi])
@@ -233,15 +262,16 @@
         own_l.wait()
         left("go", False)
         share(0)
-        r_far.start()
         own_g.wait()
         ring_g.start()
-        left("forward", False)
+        left("forward")
         ring_g.step(1)
         left("complete", False)
         share(1, 2)
+        left("across")
+        r_far.start()
         ring_g.step(2)
-        left("finish", False)
+        left("forward_far")
         share(3)
         ring_g.step(3)
         make(r_ref, rbuf.at[z, 1 - j], core, base_r + 2).wait_recv()
@@ -252,18 +282,14 @@
         share(4)
         ring_g.finish()
         rotate(1 - h, 3, 6)
-        left("forward", True)
-        ring_r.step(1)
         take(3, 7)
         rotate(1 - h, 2, 2)
         give()
-        left("complete", True)
-        share(5, 6)
+        ring_r.step(1)
+        left("finish_far")
+        share(5, 6, 7)
+        rotate(h, 0, 8)
         ring_r.step(2)
-        rotate(h, 3, 6)
-        left("finish", True)
-        share(7)
-        rotate(h, 2, 2)
 
     @pl.when(jnp.logical_not(matched))
     def _():
@@ -271,19 +297,22 @@
         ring_g.start()
         for ring, copy in zip(ring_l, swaps):
             copy.wait_recv()
+            ring.across()
             ring.go(False)
         share(0)
+        ring_g.step(1)
+        left("forward")
+        left("second")
+        share(4)
         r_far.start()
         r_near.start()
-        ring_g.step(1)
-        left("forward", False)
-        left("second")
-        share(4)
         left("complete", False)
         share(1, 2)
         ring_g.step(2)
-        left("forward", True)
-        left("finish", False)
+        left("forward_ring")
+        for ring in ring_l:
+            for copy in ring.passed:
+                copy.wait_recv()
         share(3)
         ring_g.step(3)
         left("complete", True)
@@ -291,7 +320,9 @@
         make(r_ref, rbuf.at[z, 0], core, base_r).wait_recv()
         make(r_ref, rbuf.at[z, 1], core, base_r + 1).wait_recv()
         ring_r.start()
-        left("finish", True)
+        for ring in ring_l:
+            for copy in ring.ring:
+                copy.wait_recv()
         share(7)
         ring_g.finish()
         rotate(1 - h, 0, 8)
@@ -299,9 +330,9 @@
         ring_r.step(1)
         take(0, 1, 2, 4, 5, 6)
         rotate(h, 3, 6)
-        ring_r.step(2)
         take(3, 7)
         rotate(h, 2, 2)
+        ring_r.step(2)
 
 
     ring_rot = [RingX(rot, *r) for r in halves]
@@ -310,17 +341,17 @@
         exchange[2 * n + 1].wait_recv()
         rows = pl.ds(*r)
         rot[first, rows] = (part[h, rows] + part_in[rows]).astype(BF16)
+        ring_rot[n].across()
         ring_rot[n].go(False)
+    ring_rot[0].forward()
+    ring_rot[0].second()
     ring_r.step(3)
-    ring_rot[0].second()
-    ring_rot[0].forward(False)
+    ring_rot[1].forward()
     ring_rot[1].second()
-    ring_rot[0].forward(True)
-    ring_rot[1].forward(False)
-    ring_rot[1].forward(True)
-    for other in (False, True):
-        ring_rot[0].complete(other)
-        ring_rot[0].finish(other)
+    ring_rot[0].forward_far()
+    ring_rot[1].forward_far()
+    ring_rot[0].complete(False)
+    ring_rot[0].finish_far()
     ring_r.finish()
 
     keep_avg.wait()
@@ -331,9 +362,8 @@
     for n, r in enumerate(halves):
         rows = pl.ds(*r)
         if n == 1:
-            for other in (False, True):
-                ring_rot[1].complete(other)
-                ring_rot[1].finish(other)
+            ring_rot[1].complete(False)
+            ring_rot[1].finish_far()
         proj[:, rows] = jnp.zeros((2, 256, 256), F32)
 
         def project(q, carry):
@@ -346,16 +376,13 @@
         projected = proj[j, rows] + proj_in[rows]
         new_avg = beta_first * avg[rows] + (1.0 - beta_first) * projected
         new_sq = beta_second * sq[rows] + (1.0 - beta_second) * projected * projected
-        avg[rows] = new_avg
-        sq[rows] = new_sq
+        proj_in[rows] = projected
         dbuf[h, rows] = (
             new_avg / first_fix / (jnp.sqrt(new_sq / second_fix) + epsilon)
         ).astype(BF16)
         give_d.append(same(dbuf.at[h, rows], yl))
-    out_avg = pltpu.make_async_copy(avg, avg_out, lsem.at[3])
-    out_sq = pltpu.make_async_copy(sq, sq_out, lsem.at[4])
-    out_avg.start()
-    out_sq.start()
+    out_proj = pltpu.make_async_copy(proj_in, proj_out, lsem.at[3])
+    out_proj.start()
     for copy in give_d:
         copy.wait_recv()
 
@@ -403,95 +430,110 @@
         total += dot(hilo[n, 1].reshape(512, 256), rbuf[q, 1], NT)
         return total[:256] + total[256:]
 
-    going, kept, last = {}, {}, {}
-
-    def send(n, o, way, s, k, value):
-        rows = quarters(n)[k]
-        ssend[o, way, s, rows] = value.astype(BF16)
-        going[n, o, way, s, k] = push(
-            ssend.at[o, way, s, rows], srecv.at[o, way, s, rows], (xp, xm)[way]
+    going, last = {}, {}
+
+    def send(key, slot, n, k, value):
+        rows = pl.ds(256 * n, 256) if k is None else quarters(n)[k]
+        ssend[slot, rows] = value.astype(BF16)
+        going[key] = push(
+            ssend.at[slot, rows], srecv.at[slot, rows], yh if slot == 0 else (xp, xm)[slot % 2 == 0]
         )
 
     def part_of(value, k):
         return value[128 * k : 128 * k + 128]
 
     def up_first(n):
-        for o in (1, 0):
-            value = spread_right(n, xq(2, o == 1))
+        send((n, 0), 0, n, None, spread_right(n, xq(2, True)))
+        for way in range(2):
+            send((n, 1 + way), 1 + way, n, None, spread_right(n, xq(1 - 2 * way, True)))
+        for way in range(2):
+            value = spread_right(n, xq(1 - 2 * way, False))
+            send((n, 3 + way, 1 - way), 3 + way, n, 1 - way, part_of(value, 1 - way))
+            keep[way, quarters(n)[way]] = part_of(value, way)
+        opposite[n] = spread_right(n, xq(2, False))
+
+    def up_second(n):
+        going[n, 0].wait_recv()
+        for way in range(2):
+            rows = quarters(n)[way]
+            value = opposite[n, 128 * way : 128 * way + 128] + srecv[0, rows].astype(F32)
+            send((n, 5 + way), 5 + way, n, way, value)
+
+    def up_third(n):
+        rows = pl.ds(256 * n, 256)
+        value = spread_right(n, xq(0, True))
+        for way in range(2):
+            going[n, 1 + way].wait_recv()
+            value += srecv[1 + way, rows].astype(F32)
+        tsend[rows] = value.astype(BF16)
+        last[n] = push(tsend.at[rows], trecv.at[rows], yh)
+
+    def up_fourth(n):
+        for way in range(2):
+            rows = quarters(n)[way]
+            going[n, 5 + way].wait_recv()
+            send((n, 3 + way, way), 3 + way, n, way, keep[way, rows] + srecv[5 + way, rows].astype(F32))
+
+    def up_last(n):
+        rows = pl.ds(256 * n, 256)
+        value = spread_right(n, xq(0, False))
+        for way in range(2):
+            for k in range(2):
+                going[n, 3 + way, k].wait_recv()
+            value += srecv[3 + way, rows].astype(F32)
+        update[rows] = value
+
+    def back_open(s):
+        for n in range(2):
             for way in range(2):
-                send(n, o, way, 0, way, part_of(value, way))
-        for o in (1, 0):
-            for way in range(2):
-                value = spread_right(n, xq(1 - 2 * way, o == 1))
-                send(n, o, way, 1, 1 - way, part_of(value, 1 - way))
-                keep[o, way, quarters(n)[way]] = part_of(value, way)
-
-    def up_second(n):
-        for o in (1, 0):
-            for way in range(2):
-                rows = quarters(n)[way]
-                going[n, o, way, 0, way].wait_recv()
-                send(n, o, way, 1, way, keep[o, way, rows] + srecv[o, way, 0, rows].astype(F32))
-
-    def up_third(n, o):
-        rows = pl.ds(256 * n, 256)
-        value = spread_right(n, xq(0, o == 1))
-        for way in range(2):
-            for k in range(2):
-                going[n, o, way, 1, k].wait_recv()
-        for way in range(2):
-            value += srecv[o, way, 1, rows].astype(F32)
-        if o == 1:
-            tsend[rows] = value.astype(BF16)
-            last[n] = push(tsend.at[rows], trecv.at[rows], yh)
-        else:
-            last[n].wait_recv()
-            update[rows] = value + trecv[rows].astype(F32)
+                back_send(n, s, way, way if s == 1 else 1 - way)
 
     spread_left(zq(4))
-    for n in range(2):
-        for way in range(2):
-            back_send(n, 1, way, way)
+    back_open(1)
     spread_left(zq(3))
     spread_left(zq(-3))
-    for n in range(2):
-        for way in range(2):
-            back_send(n, 2, way, 1 - way)
+    back_open(2)
     spread_left(zq(2))
     spread_left(zq(-2))
     back_step(0, 2)
+    back_step(1, 2)
     spread_left(zq(1))
     spread_left(zq(-1))
     back_step(0, 3)
-    back_step(1, 2)
+    back_step(1, 3)
     spread_left(z)
     back_step(0, 4)
-    back_step(1, 3)
     back_step(1, 4)
     back_end(0)
     up_first(0)
-    up_second(0)
     back_end(1)
     up_first(1)
-    up_third(0, 1)
+    up_second(0)
+    up_third(0)
     up_second(1)
-    up_third(0, 0)
-    up_third(1, 1)
-    up_third(1, 0)
-    out_update = pltpu.make_async_copy(update, update_out, lsem.at[5])
-    out_update.start()
+    up_fourth(0)
+    up_third(1)
+    up_last(0)
+    up_fourth(1)
+    up_last(1)
+    out_near = pltpu.make_async_copy(update, near_out, lsem.at[4])
+    out_near.start()
+    for n in range(2):
+        last[n].wait_recv()
+    out_far = pltpu.make_async_copy(trecv, far_out, lsem.at[5])
+    out_far.start()
     drain()
-    out_avg.wait()
-    out_sq.wait()
-    out_update.wait()
+    out_proj.wait()
+    out_near.wait()
+    out_far.wait()
 
 
 def shards(grad, left_basis, right_basis, exp_avg, exp_avg_sq):
     block = jax.ShapeDtypeStruct((512, 256), F32)
     place = pl.BlockSpec(memory_space=pl.ANY)
-    return pl.pallas_call(
+    near, far, projected = pl.pallas_call(
         kernel,
-        out_shape=(block, block, block),
+        out_shape=(block, jax.ShapeDtypeStruct((512, 256), BF16), block),
         in_specs=[place] * 5,
         out_specs=(place,) * 3,
         scratch_shapes=[
@@ -511,9 +553,10 @@
             pltpu.VMEM((2, 4, 512, 256), BF16),
             pltpu.VMEM((2, 4, 512, 256), BF16),
             pltpu.VMEM((2, 2, 2, 256, 256), BF16),
-            pltpu.VMEM((2, 2, 2, 512, 256), BF16),
-            pltpu.VMEM((2, 2, 2, 512, 256), BF16),
-            pltpu.VMEM((2, 2, 512, 256), F32),
+            pltpu.VMEM((7, 512, 256), BF16),
+            pltpu.VMEM((7, 512, 256), BF16),
+            pltpu.VMEM((2, 512, 256), F32),
+            pltpu.VMEM((2, 256, 256), F32),
             pltpu.VMEM((512, 256), BF16),
             pltpu.VMEM((512, 256), BF16),
             pltpu.SemaphoreType.DMA((COPIES,)),
@@ -525,6 +568,9 @@
         ),
         cost_estimate=pl.CostEstimate(flops=6_500_000_000, bytes_accessed=4_000_000, transcendentals=0),
     )(grad, left_basis, right_basis, exp_avg, exp_avg_sq)
+    new_avg = beta_first * exp_avg + (1.0 - beta_first) * projected
+    new_sq = beta_second * exp_avg_sq + (1.0 - beta_second) * projected * projected
+    return near + far.astype(F32), new_avg, new_sq
 
 
 def solution(mesh):

time: 138 us -> 130 us (0.942); the launches traced: 136 us -> 130 us
  Pallas kernels: 131 us -> 127 us
  local copies, waits for them, and re-layouts: 3.95 us -> 0.01 us
  other arithmetic: 0 us -> 2.5 us
    pallas_call x1, Pallas kernels: 131 us -> 127 us  [shards(): pl.pallas_call(kernel, out_shape=(block, jax.ShapeDtypeStruct((512, 256),...]
    unnamed x7 -> x4, local copies, waits for them, and re-layouts: 3.95 us -> 0.01 us
    add x0 -> x1, other arithmetic: none -> 2.5 us  [shards(): beta_second * exp_avg_sq + (1.0 - beta_second) * projected * projected]
where the time goes in v3:
time: 130 us
  Pallas kernels  127 us (98%)
  other arithmetic  2.5 us (2%)
    pallas_call x1, Pallas kernels, shards(): pl.pallas_call(kernel, out_shape=(block, jax.ShapeDtypeStruct((512, 256),...  127 us

profile of v3, /device:TPU:10, one launch (start us, length us, event | category | flops | bytes accessed | tf_op | source)
XLA Modules:
  0.0 129.8 jit_solution(10583139636232372323)
XLA Ops:
  0.6 0.0 copy-start.1
  0.6 0.0 copy-start
  0.7 126.6 %shard_map.76 = (f32[512,256]{1,0:T(8,128)}, bf16[512,256]{1,0:T(8,128)(2,1)}, f32[512,256]{1,0:T(8,128)}) custom-call(bf16[512,256]{1,0:T(8,128)(2,1)} %g_ref.1, bf16[512,512]{1,0:T(8,128)(2,1)} %l_ref.1, bf16[256,256]{1,0:T(8,128)(2,1)} %r_ref.1, f32[512,256]{1,0:T(8,128)} %avg_in.1, f32[512,256]{1,0:T(8,128)} %sq_in.1), custom_call_target="tpu_custom_call" | custom-call | flops 6499999744 | bytes 4000000 | tf_op jit(solution)/shard_map/pallas_call | solution.py:534
  127.2 0.0 copy-done.1
  127.3 0.0 copy-done
  127.3 2.5 %fusion = (f32[512,256]{1,0:T(8,128)}, f32[512,256]{1,0:T(8,128)}, f32[512,256]{1,0:T(8,128)}) fusion(f32[512,256]{1,0:T(8,128)} %get-tuple-element.8, f32[512,256]{1,0:T(8,128)S(1)} %copy-done.1, f32[512,256]{1,0:T(8,128)S(1)} %copy-done, f32[512,256]{1,0:T(8,128)} %get-tuple-element.6, bf16[512,256]{1,0:T(8,128)(2,1)} %get-tuple-element.7), kind=kLoop, calls=%fused_computation.2 | loop fusion | flops 1048576 | bytes 3932160 | tf_op jit(solution)/shard_map/add | solution.py:572
Async XLA Ops:
  0.6 126.6 %copy-start.1 = (f32[512,256]{1,0:T(8,128)S(1)}, f32[512,256]{1,0:T(8,128)}, u32[]{:S(2)}) copy-start(f32[512,256]{1,0:T(8,128)} %sq_in.1) | copy-start | bytes 1572868
  0.6 126.6 %copy-start = (f32[512,256]{1,0:T(8,128)S(1)}, f32[512,256]{1,0:T(8,128)}, u32[]{:S(2)}) copy-start(f32[512,256]{1,0:T(8,128)} %avg_in.1) | copy-start | bytes 1572868

commit v4 on v3

--- a/solution.py
+++ b/solution.py
@@ -285,9 +285,9 @@
         take(3, 7)
         rotate(1 - h, 2, 2)
         give()
-        ring_r.step(1)
         left("finish_far")
         share(5, 6, 7)
+        ring_r.step(1)
         rotate(h, 0, 8)
         ring_r.step(2)
 

time: 130 us -> 129 us (level); the launches traced: 130 us -> 127 us
  Pallas kernels: 127 us -> 124 us
    pallas_call x1, Pallas kernels: 127 us -> 124 us  [shards(): pl.pallas_call(kernel, out_shape=(block, jax.ShapeDtypeStruct((512, 256),...]
where the time goes in v4:
time: 129 us; the launch traced here: 127 us
  Pallas kernels  124 us (96%)
  other arithmetic  2.5 us (2%)
    pallas_call x1, Pallas kernels, shards(): pl.pallas_call(kernel, out_shape=(block, jax.ShapeDtypeStruct((512, 256),...  124 us

profile of v4, /device:TPU:10, one launch (start us, length us, event | category | flops | bytes accessed | tf_op | source)
XLA Modules:
  0.0 126.8 jit_solution(16677242213090662204)
XLA Ops:
  0.6 0.0 copy-start.1
  0.6 0.0 copy-start
  0.7 123.6 %shard_map.76 = (f32[512,256]{1,0:T(8,128)}, bf16[512,256]{1,0:T(8,128)(2,1)}, f32[512,256]{1,0:T(8,128)}) custom-call(bf16[512,256]{1,0:T(8,128)(2,1)} %g_ref.1, bf16[512,512]{1,0:T(8,128)(2,1)} %l_ref.1, bf16[256,256]{1,0:T(8,128)(2,1)} %r_ref.1, f32[512,256]{1,0:T(8,128)} %avg_in.1, f32[512,256]{1,0:T(8,128)} %sq_in.1), custom_call_target="tpu_custom_call" | custom-call | flops 6499999744 | bytes 4000000 | tf_op jit(solution)/shard_map/pallas_call | solution.py:534
  124.3 0.0 copy-done.1
  124.3 0.0 copy-done
  124.3 2.5 %fusion = (f32[512,256]{1,0:T(8,128)}, f32[512,256]{1,0:T(8,128)}, f32[512,256]{1,0:T(8,128)}) fusion(f32[512,256]{1,0:T(8,128)} %get-tuple-element.8, f32[512,256]{1,0:T(8,128)S(1)} %copy-done.1, f32[512,256]{1,0:T(8,128)S(1)} %copy-done, f32[512,256]{1,0:T(8,128)} %get-tuple-element.6, bf16[512,256]{1,0:T(8,128)(2,1)} %get-tuple-element.7), kind=kLoop, calls=%fused_computation.2 | loop fusion | flops 1048576 | bytes 3932160 | tf_op jit(solution)/shard_map/add | solution.py:572
Async XLA Ops:
  0.6 123.7 %copy-start.1 = (f32[512,256]{1,0:T(8,128)S(1)}, f32[512,256]{1,0:T(8,128)}, u32[]{:S(2)}) copy-start(f32[512,256]{1,0:T(8,128)} %sq_in.1) | copy-start | bytes 1572868
  0.6 123.7 %copy-start = (f32[512,256]{1,0:T(8,128)S(1)}, f32[512,256]{1,0:T(8,128)}, u32[]{:S(2)}) copy-start(f32[512,256]{1,0:T(8,128)} %avg_in.1) | copy-start | bytes 1572868

commit v5 on v4

--- a/solution.py
+++ b/solution.py
@@ -350,8 +350,6 @@
     ring_rot[1].second()
     ring_rot[0].forward_far()
     ring_rot[1].forward_far()
-    ring_rot[0].complete(False)
-    ring_rot[0].finish_far()
     ring_r.finish()
 
     keep_avg.wait()
@@ -361,17 +359,21 @@
     give_d = []
     for n, r in enumerate(halves):
         rows = pl.ds(*r)
-        if n == 1:
-            ring_rot[1].complete(False)
-            ring_rot[1].finish_far()
         proj[:, rows] = jnp.zeros((2, 256, 256), F32)
 
-        def project(q, carry):
-            for c in range(2):
-                proj[c, rows] += dot(rot[q, rows], rbuf[q, c], NN)
-            return carry
-
-        lax.fori_loop(0, 8, project, 0)
+        def project(other):
+            def body(m, carry):
+                q = 2 * ((x + m) % 4) + (1 - t if other else t)
+                for c in range(2):
+                    proj[c, rows] += dot(rot[q, rows], rbuf[q, c], NN)
+                return carry
+
+            lax.fori_loop(0, 4, body, 0)
+
+        ring_rot[n].complete(False)
+        project(False)
+        ring_rot[n].finish_far()
+        project(True)
         push(proj.at[1 - j, rows], proj_in.at[rows], core).wait_recv()
         projected = proj[j, rows] + proj_in[rows]
         new_avg = beta_first * avg[rows] + (1.0 - beta_first) * projected

time: 129 us -> 128 us (level); the launches traced: 127 us -> 127 us
  no operation moved by 1% of the time
where the time goes in v5:
time: 128 us; the launch traced here: 127 us
  Pallas kernels  124 us (97%)
  other arithmetic  2.5 us (2%)
    pallas_call x1, Pallas kernels, shards(): pl.pallas_call(kernel, out_shape=(block, jax.ShapeDtypeStruct((512, 256),...  124 us

profile of v5, /device:TPU:10, one launch (start us, length us, event | category | flops | bytes accessed | tf_op | source)
XLA Modules:
  0.0 127.4 jit_solution(18311403495089037500)
XLA Ops:
  0.6 0.0 copy-start.1
  0.6 0.0 copy-start
  0.7 124.2 %shard_map.76 = (f32[512,256]{1,0:T(8,128)}, bf16[512,256]{1,0:T(8,128)(2,1)}, f32[512,256]{1,0:T(8,128)}) custom-call(bf16[512,256]{1,0:T(8,128)(2,1)} %g_ref.1, bf16[512,512]{1,0:T(8,128)(2,1)} %l_ref.1, bf16[256,256]{1,0:T(8,128)(2,1)} %r_ref.1, f32[512,256]{1,0:T(8,128)} %avg_in.1, f32[512,256]{1,0:T(8,128)} %sq_in.1), custom_call_target="tpu_custom_call" | custom-call | flops 6499999744 | bytes 4000000 | tf_op jit(solution)/shard_map/pallas_call | solution.py:536
  124.9 0.0 copy-done.1
  124.9 0.0 copy-done
  124.9 2.5 %fusion = (f32[512,256]{1,0:T(8,128)}, f32[512,256]{1,0:T(8,128)}, f32[512,256]{1,0:T(8,128)}) fusion(f32[512,256]{1,0:T(8,128)} %get-tuple-element.8, f32[512,256]{1,0:T(8,128)S(1)} %copy-done.1, f32[512,256]{1,0:T(8,128)S(1)} %copy-done, f32[512,256]{1,0:T(8,128)} %get-tuple-element.6, bf16[512,256]{1,0:T(8,128)(2,1)} %get-tuple-element.7), kind=kLoop, calls=%fused_computation.2 | loop fusion | flops 1048576 | bytes 3932160 | tf_op jit(solution)/shard_map/add | solution.py:574
Async XLA Ops:
  0.6 124.3 %copy-start.1 = (f32[512,256]{1,0:T(8,128)S(1)}, f32[512,256]{1,0:T(8,128)}, u32[]{:S(2)}) copy-start(f32[512,256]{1,0:T(8,128)} %sq_in.1) | copy-start | bytes 1572868
  0.6 124.3 %copy-start = (f32[512,256]{1,0:T(8,128)S(1)}, f32[512,256]{1,0:T(8,128)}, u32[]{:S(2)}) copy-start(f32[512,256]{1,0:T(8,128)} %avg_in.1) | copy-start | bytes 1572868

commit v6 on v5

--- a/solution.py
+++ b/solution.py
@@ -247,6 +247,14 @@
             return carry
 
         lax.fori_loop(0, number, body, 0)
+
+    def rotate_own(other):
+        def body(m, carry):
+            q = 2 * ((x + m) % 4) + (1 - t if other else t)
+            part[h] += dot(lbuf[h, q], gbuf[q], TN)
+            return carry
+
+        lax.fori_loop(0, 4, body, 0)
 
     pieces = tuple((128 * n, 128) for n in range(4))
     exchange = [later(part.at[1 - h, pl.ds(*r)], part_in.at[pl.ds(*r)], yl) for r in pieces]
@@ -285,10 +293,11 @@
         take(3, 7)
         rotate(1 - h, 2, 2)
         give()
+        rotate_own(False)
         left("finish_far")
         share(5, 6, 7)
         ring_r.step(1)
-        rotate(h, 0, 8)
+        rotate_own(True)
         ring_r.step(2)
 
     @pl.when(jnp.logical_not(matched))
@@ -328,10 +337,10 @@
         rotate(1 - h, 0, 8)
         give()
         ring_r.step(1)
-        take(0, 1, 2, 4, 5, 6)
-        rotate(h, 3, 6)
-        take(3, 7)
-        rotate(h, 2, 2)
+        take(0, 1, 2, 3)
+        rotate_own(False)
+        take(4, 5, 6, 7)
+        rotate_own(True)
         ring_r.step(2)
 
 

time: 128 us -> 127 us (level)
  no operation moved by 1% of the time
where the time goes in v6:
time: 127 us
  Pallas kernels  124 us (98%)
  other arithmetic  2.5 us (2%)
    pallas_call x1, Pallas kernels, shards(): pl.pallas_call(kernel, out_shape=(block, jax.ShapeDtypeStruct((512, 256),...  124 us

profile of v6, /device:TPU:10, one launch (start us, length us, event | category | flops | bytes accessed | tf_op | source)
XLA Modules:
  0.0 127.4 jit_solution(16096778804658555555)
XLA Ops:
  0.6 0.0 copy-start.1
  0.6 0.0 copy-start
  0.7 124.2 %shard_map.76 = (f32[512,256]{1,0:T(8,128)}, bf16[512,256]{1,0:T(8,128)(2,1)}, f32[512,256]{1,0:T(8,128)}) custom-call(bf16[512,256]{1,0:T(8,128)(2,1)} %g_ref.1, bf16[512,512]{1,0:T(8,128)(2,1)} %l_ref.1, bf16[256,256]{1,0:T(8,128)(2,1)} %r_ref.1, f32[512,256]{1,0:T(8,128)} %avg_in.1, f32[512,256]{1,0:T(8,128)} %sq_in.1), custom_call_target="tpu_custom_call" | custom-call | flops 6499999744 | bytes 4000000 | tf_op jit(solution)/shard_map/pallas_call | solution.py:545
  124.8 0.0 copy-done.1
  124.8 0.0 copy-done
  124.9 2.5 %fusion = (f32[512,256]{1,0:T(8,128)}, f32[512,256]{1,0:T(8,128)}, f32[512,256]{1,0:T(8,128)}) fusion(f32[512,256]{1,0:T(8,128)} %get-tuple-element.8, f32[512,256]{1,0:T(8,128)S(1)} %copy-done.1, f32[512,256]{1,0:T(8,128)S(1)} %copy-done, f32[512,256]{1,0:T(8,128)} %get-tuple-element.6, bf16[512,256]{1,0:T(8,128)(2,1)} %get-tuple-element.7), kind=kLoop, calls=%fused_computation.2 | loop fusion | flops 1048576 | bytes 3932160 | tf_op jit(solution)/shard_map/add | solution.py:583
Async XLA Ops:
  0.6 124.2 %copy-start.1 = (f32[512,256]{1,0:T(8,128)S(1)}, f32[512,256]{1,0:T(8,128)}, u32[]{:S(2)}) copy-start(f32[512,256]{1,0:T(8,128)} %sq_in.1) | copy-start | bytes 1572868
  0.6 124.2 %copy-start = (f32[512,256]{1,0:T(8,128)S(1)}, f32[512,256]{1,0:T(8,128)}, u32[]{:S(2)}) copy-start(f32[512,256]{1,0:T(8,128)} %avg_in.1) | copy-start | bytes 1572868
